TPU v7x, 32 devices: a whole 2x2x4 slice. The times are simulated.
32 devices in a mesh: batch: 2 (over x), head: 2 (over y), blk: 8 (over z, core).
Axes of the slice: x: 2, y: 2, z: 4, core: 2. Of those that a mesh axis runs over, the one named last changes fastest.
Arguments:
- tokens: bfloat16 [16, 2048, 1024], P(('batch', 'blk'), 'head'), parts along dimension 0, may hold values from -10.5 to 10.5
- proj_weight: bfloat16 [1024, 3072], replicated, may hold values from -0.1875 to 0.1875
- out_weight: bfloat16 [1024, 1024], replicated, may hold values from -1.5 to 1.5
- pattern: int32 [256, 16], P(('batch', 'blk')), parts along dimension 0, may hold values from 0 to 127, as said below
Outputs:
- mixed_out: bfloat16 [16, 2048, 1024], P(('batch', 'blk'), 'head'), parts along dimension 0
There are 2 independent parts, one for each index of `batch`. A program takes and returns all parts, laid end to end along the dimension named above; an argument that names none is the same for every part. Nothing has to cross between parts.
Inputs may be any that keep to these rules, and one draw needn't show every extreme that they name: `pattern`: row i lists first 6 distinct blocks j with |j - i| <= 8, among them i itself, then 10 distinct summary blocks j (j % 16 >= 12) with |j - i| > 8. Every row with 8 <= i < 120 lists i - 8 and i + 8.
All inputs are finite; a program needn't handle non-finite values.
Results may differ from a plain program's by a relative error of at most 0.0095.
Values may be sent and summed in bfloat16 or wider, within the bound.
No kernel may reach another device: no remote copies, remote signals or barrier semaphores. Data moves between devices by JAX's collectives and lax.ppermute only.
A program may use at most 128 MiB of HBM per device.

v0:
```python
import jax
import jax.numpy as jnp
from jax import lax
from jax.sharding import PartitionSpec as P

D = 1024
H = 16
HD = 64
BLK = 128
TOK_DEV = 2048
SB = 16
KSEL = 16


def on_device(tokens, proj_weight, out_weight, pattern):
    heads_axis = lax.axis_size("head")
    local_heads = H // heads_axis
    head_width = local_heads * HD
    col_width = local_heads * 3 * HD
    own_rows = tokens[0]
    local_tokens = own_rows.shape[0]
    start_col = lax.axis_index("head") * col_width
    columns = lax.dynamic_slice_in_dim(proj_weight, start_col, col_width, 1)
    columns = columns.reshape(D, local_heads, 3, HD).transpose(0, 2, 1, 3).reshape(D, col_width)
    projected = jnp.dot(
        lax.all_gather(own_rows, "head", axis=0, tiled=True),
        columns,
        preferred_element_type=jnp.float32,
    ).astype(jnp.bfloat16)
    queries = projected[:, :head_width]
    key_value = projected[:, head_width:]
    source = lax.all_gather(key_value, "blk", axis=0, tiled=True)
    source_blocks = source.reshape(-1, BLK, 2 * head_width)
    group_size = 4
    group_count = SB // group_size
    query_groups = queries.reshape(group_count, group_size, BLK, head_width)
    position_groups = pattern.reshape(group_count, group_size, KSEL)
    score_scale = HD ** (-0.5)
    lane_head = lax.broadcasted_iota(jnp.int32, (1, 1, head_width), 2) // HD

    def attend(operands):
        query_group, positions = operands
        picked = source_blocks[positions].reshape(group_size, KSEL * BLK, 2 * head_width)
        key_rows = picked[:, :, :head_width]
        value_rows = picked[:, :, head_width:]
        total = jnp.zeros((group_size, BLK, head_width), jnp.float32)
        for which in range(local_heads):
            inside = lane_head == which
            masked = jnp.where(inside, query_group, jnp.zeros_like(query_group))
            scores = (
                jnp.einsum("gqc,gkc->gqk", masked, key_rows, preferred_element_type=jnp.float32)
                * score_scale
            )
            row_max = jnp.max(scores, axis=-1, keepdims=True)
            raised = jnp.exp(scores - row_max)
            weights = (raised / jnp.sum(raised, axis=-1, keepdims=True)).astype(jnp.bfloat16)
            product = jnp.einsum(
                "gqk,gkc->gqc", weights, value_rows, preferred_element_type=jnp.float32
            )
            total = total + jnp.where(inside, product, 0.0)
        return total.astype(jnp.bfloat16)

    attended = lax.map(attend, (query_groups, position_groups))
    attended = attended.reshape(TOK_DEV, head_width)
    token_heads = lax.all_to_all(attended, "head", split_axis=0, concat_axis=1, tiled=True)
    mixed_out = jnp.dot(token_heads, out_weight, preferred_element_type=jnp.float32).astype(
        jnp.bfloat16
    )
    return mixed_out.reshape(1, local_tokens, D)


def solution(mesh):
    return jax.shard_map(
        on_device,
        mesh=mesh,
        in_specs=(P(("batch", "blk"), "head", None), P(), P(), P(("batch", "blk"), None)),
        out_specs=P(("batch", "blk"), "head", None),
        check_vma=False,
    )
```

profile of v0, /device:TPU:11, one launch (start us, length us, event | category | flops | bytes accessed | tf_op | source)
XLA Modules:
  0.0 1140.4 jit_solution(15507038387284575664)
XLA Ops:
  20.3 46.6 %all-gather.6.cloned.1.call-done = bf16[1,2048,1024]{2,1,0:T(8,128)(2,1)} async-done(((bf16[1,1024,1024]{2,1,0:T(8,128)(2,1)}), bf16[1,2048,1024]{2,1,0:T(8,128)(2,1)}) %all-gather.6.cloned.1.call-update) | async-done | bytes 4194320 | tf_op jit(solution)/shard_map/all_gather | solution.py:26
  66.8 9.6 fusion.224
  88.8 279.4 %all-gather.4.cloned.1.call-done = bf16[16384,1024]{0,1:T(8,128)(2,1)} async-done(((bf16[2048,1024]{0,1:T(8,128)(2,1)}), bf16[16384,1024]{0,1:T(8,128)(2,1)}) %all-gather.4.cloned.1.call-update) | async-done | bytes 33554448 | tf_op jit(solution)/shard_map/all_gather | solution.py:32
  368.2 44.0 %copy.17 = bf16[16384,1024]{1,0:T(8,128)(2,1)} copy(bf16[16384,1024]{0,1:T(8,128)(2,1)} %all-gather.4.cloned.1.call-done) | data formatting | bytes 67108864
  412.2 682.0 %while.12 = (s32[]{:T(128)}, bf16[4,4,128,512]{3,2,1,0:T(8,128)(2,1)}, bf16[4,4,128,512]{3,2,1,0:T(8,128)(2,1)}, s32[4,4,16]{2,1,0:T(4,128)}, bf16[128,128,1024]{2,1,0:T(8,128)(2,1)}, /*index=5*/s32[]{:T(128)}) while((s32[]{:T(128)}, bf16[4,4,128,512]{3,2,1,0:T(8,128)(2,1)}, bf16[4,4,128,512]{3,2,1,0:T(8,128)(2,1)}, ...), condition=%wide.region_17.18_spmd.clone.clone, body=%wide.region_0.17_spmd.clone.clone.sunk | while | flops 17244952576 | bytes 317245120 | solution.py:63
  436.2 13.6 %gather_fusion = bf16[64,128,1024]{2,1,0:T(8,128)(2,1)} fusion(bf16[128,128,1024]{2,1,0:T(8,128)(2,1)} %get-tuple-element.197, s32[1024]{0:T(1024)S(1)} %pad_clamp_fusion.2), kind=kCustom, calls=%fused_computation.clone.clone.1 | custom fusion | bytes 33554688 | tf_op jit(solution)/shard_map/while/body/eval_jaxpr/gather | solution.py:43
  466.8 8.4 fusion.312
  485.3 8.4 fusion.315
  523.8 8.4 fusion.321
  543.1 8.4 fusion.324
  562.4 8.4 fusion.327
  580.9 8.4 fusion.330
  600.7 12.4 %gather_fusion = bf16[64,128,1024]{2,1,0:T(8,128)(2,1)} fusion(bf16[128,128,1024]{2,1,0:T(8,128)(2,1)} %get-tuple-element.197, s32[1024]{0:T(1024)S(1)} %pad_clamp_fusion.2), kind=kCustom, calls=%fused_computation.clone.clone.1 | custom fusion | bytes 33554688 | tf_op jit(solution)/shard_map/while/body/eval_jaxpr/gather | solution.py:43
  630.0 8.4 fusion.312
  648.5 8.4 fusion.315
  687.1 8.4 fusion.321
  706.4 8.4 fusion.324
  725.7 8.4 fusion.327
  764.0 13.2 %gather_fusion = bf16[64,128,1024]{2,1,0:T(8,128)(2,1)} fusion(bf16[128,128,1024]{2,1,0:T(8,128)(2,1)} %get-tuple-element.197, s32[1024]{0:T(1024)S(1)} %pad_clamp_fusion.2), kind=kCustom, calls=%fused_computation.clone.clone.1 | custom fusion | bytes 33554688 | tf_op jit(solution)/shard_map/while/body/eval_jaxpr/gather | solution.py:43
  794.2 8.4 fusion.312
  812.7 8.4 fusion.315
  851.2 8.4 fusion.321
  870.5 8.4 fusion.324
  889.8 8.4 fusion.327
  908.3 8.4 fusion.330
  928.1 13.4 %gather_fusion = bf16[64,128,1024]{2,1,0:T(8,128)(2,1)} fusion(bf16[128,128,1024]{2,1,0:T(8,128)(2,1)} %get-tuple-element.197, s32[1024]{0:T(1024)S(1)} %pad_clamp_fusion.2), kind=kCustom, calls=%fused_computation.clone.clone.1 | custom fusion | bytes 33554688 | tf_op jit(solution)/shard_map/while/body/eval_jaxpr/gather | solution.py:43
  958.5 8.4 fusion.312
  977.0 8.4 fusion.315
  1015.5 8.4 fusion.321
  1034.8 8.4 fusion.324
  1054.1 8.4 fusion.327
  1094.2 29.9 %all_to_all.19 = bf16[2,1024,512]{2,1,0:T(8,128)(2,1)} all-to-all(bf16[2,1024,512]{2,1,0:T(8,128)(2,1)} %bitcast.89), channel_id=1, replica_groups=mesh['batch'=2,'head'=2,'blk'=8] {'head'}, dimensions={0} | all-to-all | bytes 4194304 | tf_op jit(solution)/shard_map/all_to_all | solution.py:65
  (167 shorter events, 453.6 us)
Async XLA Ops:
  6.5 1121.5 %copy-start = (bf16[1024,1024]{1,0:T(8,128)(2,1)S(1)}, bf16[1024,1024]{1,0:T(8,128)(2,1)}, u32[]{:S(2)}) copy-start(bf16[1024,1024]{1,0:T(8,128)(2,1)} %param.8) | copy-start | bytes 6291460
  6.5 60.3 %all-gather.6.cloned.1.call-start = ((), (), s32[]{:S(2)}) async-start(), calls=%async_computation.2 | async-start | bytes 6291456 | tf_op jit(solution)/shard_map/all_gather | solution.py:26
  7.3 360.9 %all-gather.4.cloned.1.call-start = ((), (), s32[]{:S(2)}) async-start(), calls=%async_computation.1 | async-start | bytes 37748736 | tf_op jit(solution)/shard_map/all_gather | solution.py:32
  76.4 2.7 copy-start.2
  456.2 2.0 copy-start.1
  512.9 3.4 copy-start.3
  532.2 3.4 copy-start.4
  551.5 3.4 copy-start.5
  619.5 2.0 copy-start.1
  676.2 3.4 copy-start.3
  695.5 3.4 copy-start.4
  714.8 3.4 copy-start.5
  783.6 2.0 copy-start.1
  840.3 3.4 copy-start.3
  859.6 3.4 copy-start.4
  878.9 3.4 copy-start.5
  947.9 2.0 copy-start.1
  1004.6 3.4 copy-start.3
  1023.9 3.4 copy-start.4
  1043.2 3.4 copy-start.5
Sparse Core Ops, SparseCore 0:
  8.9 57.8 all-gather.5
  81.9 286.2 all-gather.3
where the time goes:
time: 1150 us; the launch traced here: 1140 us
  matrix products  507 us (44%)
  waiting for transfers between devices  327 us (28%)
  local copies, waits for them, and re-layouts  134 us (12%)
  other arithmetic  103 us (9%)
  blocking collectives  29.9 us (3%)
  loops' own time  26 us (2%)
  between operations  13.6 us (1%)
    all_gather x1, waiting for transfers between devices, on_device(): source = lax.all_gather(key_value, 'blk', axis=0, tiled=True)  279 us
    dot_general x32, matrix products, attend(): jnp.einsum('gqc,gkc->gqk', masked, key_rows, preferred_element_type=jnp.f...  261 us
    dot_general x32, matrix products, attend(): jnp.einsum('gqk,gkc->gqc', weights, value_rows, preferred_element_type=jn...  231 us
    sub x32, other arithmetic, attend(): raised = jnp.exp(scores - row_max)  99 us
    unnamed x7, local copies, waits for them, and re-layouts  55.2 us
    gather x4, local copies, waits for them, and re-layouts, attend(): source_blocks[positions].reshape(group_size, KSEL * BLK, 2 * head_width)  52.5 us
    all_gather x1, waiting for transfers between devices, on_device(): lax.all_gather(own_rows, 'head', axis=0, tiled=True)  46.6 us
    all_to_all x1, blocking collectives, on_device(): lax.all_to_all(attended, 'head', split_axis=0, concat_axis=1, tiled=True)  29.9 us
  transfers between devices with their start and end apart: 2, of which 2 were waited for; matrix products, arithmetic and copies ran while one was open for 2% of the time, Pallas kernels for 0%

commit v1 on v0

v1 whole, which is shorter than its diff:
```python
import functools

import jax
import jax.numpy as jnp
from jax import lax
from jax.experimental import pallas as pl
from jax.experimental.pallas import tpu as pltpu
from jax.sharding import PartitionSpec as P

D = 1024
H = 16
HD = 64
BLK = 128
REACH = 8
LSEL = 6
SUMB = 4
SB = 16
KSEL = 16
PAIRS = H // 2
LANES = 2 * HD
LOG2E = 1.4426950408889634
TOTAL_CAP = 2.0**100


def split_kernel(weight_ref, query_ref, key_ref, value_ref):
    both = weight_ref[...]
    first, second = both[:, : 3 * HD], both[:, 3 * HD :]

    def columns(which):
        lo = which * HD
        return jnp.concatenate([first[:, lo : lo + HD], second[:, lo : lo + HD]], axis=1)

    query_ref[...] = columns(0).T
    key_ref[...] = columns(1)
    value_ref[...] = columns(2).T


def split_weights(proj_weight):
    wide = jax.ShapeDtypeStruct((D, D), jnp.bfloat16)
    across = pl.BlockSpec((LANES, D), lambda p: (p, 0))
    down = pl.BlockSpec((D, LANES), lambda p: (0, p))
    return pl.pallas_call(
        split_kernel,
        grid=(PAIRS,),
        in_specs=[pl.BlockSpec((D, 3 * LANES), lambda p: (0, p))],
        out_specs=[across, down, across],
        out_shape=[wide, wide, wide],
        cost_estimate=pl.CostEstimate(flops=0, bytes_accessed=4 * D * 3 * D, transcendentals=0),
        name="split_weights",
    )(proj_weight)


def attend_kernel(
    blocks, table_ref, query_ref, near_key_ref, near_value_ref, far_key_ref, far_value_ref, out_ref, peak_ref
):
    f32, bf16 = jnp.float32, jnp.bfloat16
    row = lax.broadcasted_iota(jnp.int32, (LANES, BLK), 0)
    ones = jnp.ones((16, 2 * BLK), bf16)

    def queries(index):
        own = query_ref[:, pl.ds(pl.multiple_of(index * BLK, BLK), BLK)]
        zero = jnp.zeros_like(own)
        return jnp.concatenate([jnp.where(row < HD, own, zero), jnp.where(row < HD, zero, own)], axis=1)

    def place(index, which):
        return pl.multiple_of(table_ref[index, which] * BLK, BLK)

    def keys(ref, index, which):
        return jnp.concatenate([ref[pl.ds(place(index, which + n), BLK), :] for n in range(2)], axis=0)

    def values(ref, index, which):
        picked = [ref[:, pl.ds(place(index, which + n), BLK)] for n in range(2)]
        return jnp.concatenate([jnp.concatenate(picked, axis=1), ones], axis=0)

    def score(ref, index, which, query):
        return jnp.dot(keys(ref, index, which), query, preferred_element_type=f32)

    def gather(ref, index, which, scores, shift):
        raised = jnp.exp2(scores - shift).astype(bf16)
        return jnp.dot(values(ref, index, which), raised, preferred_element_type=f32)

    def finish(index, total):
        scaled = total[:LANES] / total[LANES : LANES + 1]
        mine = jnp.concatenate([scaled[:HD, :BLK], scaled[HD:, BLK:]], axis=0)
        out_ref[pl.ds(pl.multiple_of(index * BLK, BLK), BLK), :] = mine.T.astype(bf16)

    def refs(which):
        return (near_key_ref, near_value_ref) if which < LSEL else (far_key_ref, far_value_ref)

    peak_ref[...] = jnp.zeros_like(peak_ref)

    def one(index):
        query = queries(index)
        total = None
        for which in range(0, KSEL, 2):
            key_ref, value_ref = refs(which)
            scores = score(key_ref, index, which, query)
            if which == 0:
                shift = jnp.max(scores, axis=0, keepdims=True)
            part = gather(value_ref, index, which, scores, shift)
            total = part if total is None else total + part
        peak_ref[...] = jnp.maximum(peak_ref[...], total[LANES : LANES + 8])
        finish(index, total)

    def step(number, carry):
        for n in range(2):
            one(2 * number + n)
        return carry

    if blocks % 2:
        lax.fori_loop(0, blocks, lambda index, carry: (one(index), carry)[1], 0)
    else:
        lax.fori_loop(0, blocks // 2, step, 0)

    @pl.when(jnp.logical_not(jnp.max(peak_ref[...]) <= TOTAL_CAP))
    def _():
        def whole_row(index, carry):
            query = queries(index)
            shift = jnp.full((1, 2 * BLK), -jnp.inf, f32)
            for which in range(0, KSEL, 2):
                scores = score(refs(which)[0], index, which, query)
                shift = jnp.maximum(shift, jnp.max(scores, axis=0, keepdims=True))
            total = jnp.zeros((LANES + 16, 2 * BLK), f32)
            for which in range(0, KSEL, 2):
                key_ref, value_ref = refs(which)
                total += gather(value_ref, index, which, score(key_ref, index, which, query), shift)
            finish(index, total)
            return carry

        lax.fori_loop(0, blocks, whole_row, 0)


def attend(table, query, near_key, near_value, far_key, far_value):
    rows = query.shape[1]
    blocks = rows // BLK
    pair_rows = lambda array: pl.BlockSpec((LANES, array.shape[1]), lambda p: (p, 0))
    pair_columns = lambda array: pl.BlockSpec((array.shape[0], LANES), lambda p: (0, p))
    scores = rows * KSEL * BLK * H
    moved = 2 * (near_key.size + near_value.size + far_key.size + far_value.size + 2 * query.size)
    return pl.pallas_call(
        functools.partial(attend_kernel, blocks),
        grid=(PAIRS,),
        in_specs=[
            pl.BlockSpec(memory_space=pltpu.SMEM),
            pair_rows(query),
            pair_columns(near_key),
            pair_rows(near_value),
            pair_columns(far_key),
            pair_rows(far_value),
        ],
        out_specs=pl.BlockSpec((rows, LANES), lambda p: (0, p)),
        out_shape=jax.ShapeDtypeStruct((rows, D), jnp.bfloat16),
        scratch_shapes=[pltpu.VMEM((8, 2 * BLK), jnp.float32)],
        compiler_params=pltpu.CompilerParams(vmem_limit_bytes=48 * 2**20),
        cost_estimate=pl.CostEstimate(
            flops=4 * scores * HD * 4, bytes_accessed=moved, transcendentals=scores
        ),
        name="attend",
    )(table, query, near_key, near_value, far_key, far_value)


def project_rows(rows, weight):
    return jnp.dot(rows, weight, preferred_element_type=jnp.float32).astype(jnp.bfloat16)


def project_columns(weight, rows, scale=None):
    wide = lax.dot_general(weight, rows, (((1,), (1,)), ((), ())), preferred_element_type=jnp.float32)
    return (wide if scale is None else wide * scale).astype(jnp.bfloat16)


def on_device(tokens, proj_weight, out_weight, pattern):
    heads = lax.axis_size("head")
    strides = lax.axis_size("blk")
    place = lax.axis_index("head")
    stride = lax.axis_index("blk")
    own = tokens[0]
    blocks = own.shape[0] // BLK
    lower = place < heads // 2

    whole = lax.all_gather(own, "head", axis=0, tiled=True)
    half = whole.shape[0] // 2
    leaving = jnp.where(lower, whole[half:], whole[:half])
    steps = []
    for h in range(heads):
        for s in range(strides - 1):
            ends = (h * strides + s, h * strides + s + 1)
            steps.append(ends if h < heads // 2 else ends[::-1])
    arriving = lax.ppermute(leaving, ("head", "blk"), steps)
    near_rows = jnp.concatenate([whole, arriving], axis=0)
    far_rows = lax.all_gather(whole[-SUMB * BLK :], "blk", axis=0, tiled=True)

    query_weight, key_weight, value_weight = split_weights(proj_weight)
    query = project_columns(query_weight, own, LOG2E * HD**-0.5)
    near_key = project_rows(near_rows, key_weight)
    near_value = project_columns(value_weight, near_rows)
    far_key = project_rows(far_rows, key_weight)
    far_value = project_columns(value_weight, far_rows)

    listed = lax.dynamic_slice_in_dim(pattern, place * blocks, blocks, 0)
    near = listed[:, :LSEL] - stride * SB
    near = jnp.where(near < 0, near + SB + REACH, near)
    far = listed[:, LSEL:]
    far = far // SB * SUMB + far % SB - (SB - SUMB)
    table = jnp.concatenate([near, far], axis=1)

    mixed = attend(table, query, near_key, near_value, far_key, far_value)
    out = project_rows(mixed, out_weight)
    return out.reshape(tokens.shape)


def solution(mesh):
    return jax.shard_map(
        on_device,
        mesh=mesh,
        in_specs=(P(("batch", "blk"), "head", None), P(), P(), P(("batch", "blk"), None)),
        out_specs=P(("batch", "blk"), "head", None),
        check_vma=False,
    )
```

time: 1150 us -> 288 us (0.25)
  matrix products: 507 us -> 58.1 us
  waiting for transfers between devices: 327 us -> 136 us
  local copies, waits for them, and re-layouts: 134 us -> 2.28 us
  other arithmetic: 103 us -> 3.91 us
  Pallas kernels: 0 us -> 69.6 us
  blocking collectives: 29.9 us -> 0 us
  loops' own time: 26 us -> 0 us
    dot_general x66 -> x6, matrix products: 507 us -> 58.1 us  [the longest x3 31.4 us: project_columns(): lax.dot_general(weight, rows, (((1,), (1,)), ((), ())), preferred_element...]
    all_gather x2, waiting for transfers between devices: 326 us -> 59.5 us  [the longest x1 59.5 us: on_device(): whole = lax.all_gather(own, 'head', axis=0, tiled=True)]
    sub x32 -> x1, other arithmetic: 99 us -> 0.09 us  [on_device(): far = far // SB * SUMB + far % SB - (SB - SUMB)]
    ppermute x0 -> x1, waiting for transfers between devices: none -> 75.9 us  [on_device(): arriving = lax.ppermute(leaving, ('head', 'blk'), steps)]
    pallas_call x0 -> x2, Pallas kernels: none -> 69.6 us  [the longest x1 61 us: attend(): pl.pallas_call(functools.partial(attend_kernel, blocks), grid=(PAIRS,), i...]
    unnamed x7 -> x14, local copies, waits for them, and re-layouts: 55.2 us -> 0.03 us
    gather x4 -> x0, local copies, waits for them, and re-layouts: 52.5 us -> none  [attend(): source_blocks[positions].reshape(group_size, KSEL * BLK, 2 * head_width)]
    all_to_all x1 -> x0, blocking collectives: 29.9 us -> none  [on_device(): lax.all_to_all(attended, 'head', split_axis=0, concat_axis=1, tiled=True)]
  transfers between devices with their start and end apart: 2 -> 3, of which waited for: 2 -> 2; matrix products, arithmetic and copies ran while one was open for 2% -> 11% of each run, Pallas kernels for 0% -> 3%
where the time goes in v1:
time: 288 us; the launch traced here: 287 us
  waiting for transfers between devices  136 us (47%)
  Pallas kernels  69.6 us (24%)
  matrix products  58.1 us (20%)
  between operations  13.4 us (5%)
  other arithmetic  3.91 us (1%)
  starting transfers between devices  3.83 us (1%)
    ppermute x1, waiting for transfers between devices, on_device(): arriving = lax.ppermute(leaving, ('head', 'blk'), steps)  75.9 us
    pallas_call x1, Pallas kernels, attend(): pl.pallas_call(functools.partial(attend_kernel, blocks), grid=(PAIRS,), i...  61 us
    all_gather x1, waiting for transfers between devices, on_device(): whole = lax.all_gather(own, 'head', axis=0, tiled=True)  59.5 us
    dot_general x3, matrix products, project_columns(): lax.dot_general(weight, rows, (((1,), (1,)), ((), ())), preferred_element...  31.4 us
    dot_general x3, matrix products, project_rows(): jnp.dot(rows, weight, preferred_element_type=jnp.float32)  26.7 us
    pallas_call x1, Pallas kernels, split_weights(): pl.pallas_call(split_kernel, grid=(PAIRS,), in_specs=[pl.BlockSpec((D, 3...  8.55 us
  transfers between devices with their start and end apart: 3, of which 2 were waited for; matrix products, arithmetic and copies ran while one was open for 11% of the time, Pallas kernels for 3%

profile of v1, /device:TPU:11, one launch (start us, length us, event | category | flops | bytes accessed | tf_op | source)
XLA Modules:
  0.0 287.3 jit_solution(5985036381576376553)
XLA Ops:
  6.5 0.0 copy-start
  6.5 0.0 all-gather.5.cloned.1.call-start
  6.5 0.7 all-gather.5.cloned.1.call-update
  7.3 0.0 all-gather.7.cloned.1.call-start
  7.3 59.5 %all-gather.5.cloned.1.call-done = bf16[1,2048,1024]{2,1,0:T(8,128)(2,1)} async-done(((bf16[1,1024,1024]{2,1,0:T(8,128)(2,1)}), bf16[1,2048,1024]{2,1,0:T(8,128)(2,1)}) %all-gather.5.cloned.1.call-update) | async-done | bytes 4194320 | tf_op jit(solution)/shard_map/all_gather | solution.py:180
  66.8 2.3 slice.25
  69.1 0.0 all-gather.7.cloned.1.call-update
  69.1 3.7 %fusion.10 = bf16[1024,1024]{1,0:T(8,128)(2,1)} fusion(bf16[1,2048,1024]{2,1,0:T(8,128)(2,1)} %all-gather.5.cloned.1.call-done, pred[]{:T(512)S(6)} %lt.22), kind=kLoop, calls=%fused_computation.11 | loop fusion | flops 1048576 | bytes 6291457 | tf_op jit(solution)/shard_map/jit(_where)/select_n | solution.py:182
  72.9 0.0 copy-start.3
  72.9 3.8 %collective-permute-start = (bf16[1024,1024]{1,0:T(8,128)(2,1)}, bf16[1024,1024]{1,0:T(8,128)(2,1)}, u32[]{:S(2)}, u32[]{:S(2)}) collective-permute-start(bf16[1024,1024]{1,0:T(8,128)(2,1)} %fusion.10), channel_id=1, source_target_pairs={{0,1},{1,2},{2,3},{3,4},{4,5},{5,6},{6,7},{9,8},{10,9},{11,10},{12... | collective-permute-start | bytes 6291464 | tf_op jit(solution)/shard_map/ppermute | solution.py:188
  76.7 8.6 %split_weights.1 = (bf16[1024,1024]{1,0:T(8,128)(2,1)}, bf16[1024,1024]{1,0:T(8,128)(2,1)}, bf16[1024,1024]{1,0:T(8,128)(2,1)}) custom-call(bf16[1024,3072]{1,0:T(8,128)(2,1)} %weight_ref.1), custom_call_target="tpu_custom_call" | custom-call | bytes 12582912 | tf_op jit(solution)/shard_map/split_weights/pallas_call | solution.py:42
  85.2 0.0 copy-done.3
  85.2 0.1 fusion.14
  85.3 0.1 pad_add_fusion.table_ref
  85.4 0.0 copy-start.2
  85.4 0.0 copy-start.6
  85.4 6.1 %multiply_convert_fusion.query_ref = bf16[1024,1024]{1,0:T(8,128)(2,1)} fusion(bf16[1024,1024]{1,0:T(8,128)(2,1)} %get-tuple-element.8, bf16[1,1024,1024]{2,1,0:T(8,128)(2,1)} %param.4), kind=kOutput, calls=%fused_computation.9 | convolution fusion | flops 2149580800 | bytes 6291456 | tf_op jit(solution)/shard_map/dot_general | solution.py:167
  91.5 75.9 %collective-permute-done = bf16[1024,1024]{1,0:T(8,128)(2,1)} collective-permute-done((bf16[1024,1024]{1,0:T(8,128)(2,1)}, bf16[1024,1024]{1,0:T(8,128)(2,1)}, u32[]{:S(2)}, u32[]{:S(2)}) %collective-permute-start) | collective-permute-done | bytes 2097184 | tf_op jit(solution)/shard_map/ppermute | solution.py:188
  167.3 0.0 copy-done.2
  167.3 0.0 copy-done.6
  167.4 0.0 copy-start.5
  167.4 10.3 %convert_bitcast_fusion.near_value_ref = bf16[1024,3072]{1,0:T(8,128)(2,1)} fusion(bf16[1024,1024]{1,0:T(8,128)(2,1)S(1)} %copy-done.6, bf16[1024,1024]{1,0:T(8,128)(2,1)} %collective-permute-done, bf16[2048,1024]{1,0:T(8,128)(2,1)S(1)} %bitcast.26), kind=kOutput, calls=%fused_computation.7 | convolution fusion | flops 6458179584 | bytes 14680064 | tf_op jit(solution)/shard_map/dot_general | solution.py:167
  177.7 0.0 copy-done.5
  177.7 10.4 %convolution_convert_fusion.near_key_ref = bf16[3072,1024]{1,0:T(8,128)(2,1)} fusion(bf16[1024,1024]{1,0:T(8,128)(2,1)S(1)} %copy-done.5, bf16[1024,1024]{1,0:T(8,128)(2,1)} %collective-permute-done, bf16[2048,1024]{1,0:T(8,128)(2,1)S(1)} %bitcast.27), kind=kOutput, calls=%fused_computation.8 | convolution fusion | flops 6458179584 | bytes 14680064 | tf_op jit(solution)/shard_map/dot_general | solution.py:163
  188.1 0.0 all-gather.7.cloned.1.call-done
  188.1 15.1 %fusion.7.far_value_ref = bf16[1024,4096]{1,0:T(8,128)(2,1)} fusion(bf16[1024,1024]{1,0:T(8,128)(2,1)} %get-tuple-element.10, bf16[1,4096,1024]{2,1,0:T(8,128)(2,1)} %all-gather.7.cloned.1.call-done), kind=kOutput, calls=%fused_computation.5 | convolution fusion | flops 8594128896 | bytes 18874368 | tf_op jit(solution)/shard_map/dot_general | solution.py:167
  203.2 0.0 copy-done.4
  203.2 12.6 %fusion.4.far_key_ref = bf16[4096,1024]{1,0:T(8,128)(2,1)} fusion(bf16[1024,1024]{1,0:T(8,128)(2,1)} %get-tuple-element.9, bf16[1,4096,1024]{2,1,0:T(8,128)(2,1)S(1)} %copy-done.4), kind=kOutput, calls=%fused_computation.4 | convolution fusion | flops 8594128896 | bytes 18874368 | tf_op jit(solution)/shard_map/dot_general | solution.py:163
  215.8 0.0 copy-done.1
  215.8 61.0 %attend.1 = bf16[1024,1024]{1,0:T(8,128)(2,1)S(1)} custom-call(s32[8,16]{1,0:T(8,128)S(1)} %pad_add_fusion.table_ref, bf16[1024,1024]{1,0:T(8,128)(2,1)S(1)} %copy-done.1, bf16[3072,1024]{1,0:T(8,128)(2,1)} %convolution_convert_fusion.near_key_ref, bf16[1024,3072]{1,0:T(8,128)(2,1)} %convert_bitcast_fusion.near_value_ref, ...), custom_call_target="tpu_custom_call" | custom-call | flops 34359738368 | bytes 33554432 | tf_op jit(solution)/shard_map/attend/pallas_call | solution.py:140
  276.8 0.0 copy-done
  276.8 3.7 %convert_bitcast_fusion.1 = bf16[1,1024,1024]{2,1,0:T(8,128)(2,1)} fusion(bf16[1024,1024]{1,0:T(8,128)(2,1)S(1)} %attend.1, bf16[1024,1024]{1,0:T(8,128)(2,1)S(1)} %copy-done), kind=kOutput, calls=%fused_computation.13 | convolution fusion | flops 2148532224 | bytes 6291456 | tf_op jit(solution)/shard_map/dot_general | solution.py:163
  (4 shorter events, 0.0 us)
Async XLA Ops:
  6.5 270.2 %copy-start = (bf16[1024,1024]{1,0:T(8,128)(2,1)S(1)}, bf16[1024,1024]{1,0:T(8,128)(2,1)}, u32[]{:S(2)}) copy-start(bf16[1024,1024]{1,0:T(8,128)(2,1)} %param.6) | copy-start | bytes 6291460
  6.5 60.3 %all-gather.5.cloned.1.call-start = ((), (), s32[]{:S(2)}) async-start(), calls=%async_computation | async-start | bytes 6291456 | tf_op jit(solution)/shard_map/all_gather | solution.py:180
  7.3 180.9 %all-gather.7.cloned.1.call-start = ((), (), s32[]{:S(2)}) async-start(), calls=%async_computation.1 | async-start | bytes 9437184 | tf_op jit(solution)/shard_map/all_gather | solution.py:190
  72.9 12.4 %copy-start.3 = (s32[16,16]{1,0:T(8,128)S(1)}, s32[16,16]{1,0:T(8,128)}, u32[]{:S(2)}) copy-start(s32[16,16]{1,0:T(8,128)} %param.7) | copy-start | bytes 3076
  72.9 94.5 %collective-permute-start = (bf16[1024,1024]{1,0:T(8,128)(2,1)}, bf16[1024,1024]{1,0:T(8,128)(2,1)}, u32[]{:S(2)}, u32[]{:S(2)}) collective-permute-start(bf16[1024,1024]{1,0:T(8,128)(2,1)} %fusion.10), channel_id=1, source_target_pairs={{0,1},{1,2},{2,3},{3,4},{4,5},{5,6},{6,7},{9,8},{10,9},{11,10},{12... | collective-permute-start | bytes 6291464 | tf_op jit(solution)/shard_map/ppermute | solution.py:188
  85.4 82.0 %copy-start.2 = (bf16[1,2048,1024]{2,1,0:T(8,128)(2,1)S(1)}, bf16[1,2048,1024]{2,1,0:T(8,128)(2,1)}, u32[]{:S(2)}) copy-start(bf16[1,2048,1024]{2,1,0:T(8,128)(2,1)} %all-gather.5.cloned.1.call-done) | copy-start | bytes 12582916
  85.4 82.0 %copy-start.6 = (bf16[1024,1024]{1,0:T(8,128)(2,1)S(1)}, bf16[1024,1024]{1,0:T(8,128)(2,1)}, u32[]{:S(2)}) copy-start(bf16[1024,1024]{1,0:T(8,128)(2,1)} %get-tuple-element.10) | copy-start | bytes 6291460
  167.4 10.3 %copy-start.5 = (bf16[1024,1024]{1,0:T(8,128)(2,1)S(1)}, bf16[1024,1024]{1,0:T(8,128)(2,1)}, u32[]{:S(2)}) copy-start(bf16[1024,1024]{1,0:T(8,128)(2,1)} %get-tuple-element.9) | copy-start | bytes 6291460
  188.1 15.1 %copy-start.4 = (bf16[1,4096,1024]{2,1,0:T(8,128)(2,1)S(1)}, bf16[1,4096,1024]{2,1,0:T(8,128)(2,1)}, u32[]{:S(2)}) copy-start(bf16[1,4096,1024]{2,1,0:T(8,128)(2,1)} %all-gather.7.cloned.1.call-done) | copy-start | bytes 25165828
  203.2 12.6 %copy-start.1 = (bf16[1024,1024]{1,0:T(8,128)(2,1)S(1)}, bf16[1024,1024]{1,0:T(8,128)(2,1)}, u32[]{:S(2)}) copy-start(bf16[1024,1024]{1,0:T(8,128)(2,1)} %multiply_convert_fusion.query_ref) | copy-start | bytes 6291460
Sparse Core Ops, SparseCore 0:
  8.9 57.8 all-gather.4
  69.2 100.9 all-gather.6

commit v2 on v0

v2 whole, which is shorter than its diff:
```python
import functools

import jax
import jax.numpy as jnp
from jax import lax
from jax.experimental import pallas as pl
from jax.experimental.pallas import tpu as pltpu
from jax.sharding import PartitionSpec as P

D = 1024
H = 16
HD = 64
BLK = 128
REACH = 8
LSEL = 6
SUMB = 4
SB = 16
KSEL = 16
PAIRS = H // 2
LANES = 2 * HD
TILE = 512
TOTAL_CAP = 2.0**100


def split_kernel(weight_ref, query_ref, both_ref):
    both = weight_ref[...]
    first, second = both[:, : 3 * HD], both[:, 3 * HD :]

    def columns(which):
        lo = which * HD
        return jnp.concatenate([first[:, lo : lo + HD], second[:, lo : lo + HD]], axis=1)

    query_ref[...] = columns(0).T
    both_ref[...] = jnp.concatenate([columns(1), columns(2)], axis=1)


def split_weights(proj_weight):
    return pl.pallas_call(
        split_kernel,
        grid=(PAIRS,),
        in_specs=[pl.BlockSpec((D, 3 * LANES), lambda p: (0, p))],
        out_specs=[pl.BlockSpec((LANES, D), lambda p: (p, 0)), pl.BlockSpec((D, 2 * LANES), lambda p: (0, p))],
        out_shape=[jax.ShapeDtypeStruct((D, D), jnp.bfloat16), jax.ShapeDtypeStruct((D, 2 * D), jnp.bfloat16)],
        cost_estimate=pl.CostEstimate(flops=0, bytes_accessed=4 * D * 3 * D, transcendentals=0),
        name="split_weights",
    )(proj_weight)


def attend_kernel(first, last, blocks, count, sources, *refs):
    f32, bf16 = jnp.float32, jnp.bfloat16
    refs = list(refs)
    table_ref, query_ref, weight_ref = refs[:3]
    source_refs = refs[3 : 3 + sources]
    refs = refs[3 + sources :]
    if not first:
        sum_in_ref, row_in_ref = refs[:2]
        refs = refs[2:]
    if last:
        out_ref = refs.pop(0)
    else:
        sum_out_ref, row_out_ref = refs[:2]
        refs = refs[2:]
    slots = [(refs[0], refs[1]), (refs[2], refs[3])]

    row = lax.broadcasted_iota(jnp.int32, (LANES, BLK), 0)
    ones = jnp.ones((16, 2 * BLK), bf16)

    def at(index, size=BLK):
        return pl.ds(pl.multiple_of(index * size, size), size)

    def project_rows(pair, pieces, slot):
        key_ref, value_ref = slot
        weight = weight_ref[:, at(pair, 2 * LANES)]
        parts = [ref[pl.ds(start, size), :] for ref, start, size, _ in pieces]
        rows = parts[0] if len(parts) == 1 else jnp.concatenate(parts, axis=0)
        both = jnp.dot(rows, weight, preferred_element_type=f32).astype(bf16)
        done = 0
        for _, _, size, target in pieces:
            part = both[done : done + size]
            key_ref[pl.ds(target, size), :] = part[:, :LANES]
            value_ref[:, pl.ds(target, size)] = part[:, LANES:].T
            done += size

    def project(pair, index, slot):
        offset = 0
        small = []
        for ref in source_refs:
            size = ref.shape[0] // blocks
            start = pl.multiple_of(index * size, BLK)
            if size <= TILE:
                small.append((ref, start, size, pl.multiple_of(offset + start, BLK)))
            else:

                def tile(n, carry, ref=ref, start=start, offset=offset):
                    begin = pl.multiple_of(start + n * TILE, BLK)
                    project_rows(pair, [(ref, begin, TILE, pl.multiple_of(offset + begin, BLK))], slot)
                    return carry

                lax.fori_loop(0, size // TILE, tile, 0)
            offset += ref.shape[0]
        if small:
            project_rows(pair, small, slot)

    def queries(half, index):
        own = query_ref[half * LANES : (half + 1) * LANES, at(index)]
        zero = jnp.zeros_like(own)
        return jnp.concatenate([jnp.where(row < HD, own, zero), jnp.where(row < HD, zero, own)], axis=1)

    def places(index, which):
        return [pl.multiple_of(table_ref[index, which + n] * BLK, BLK) for n in range(2)]

    def score(slot, index, which, query):
        keys = [slot[0][pl.ds(place, BLK), :] for place in places(index, which)]
        return jnp.dot(jnp.concatenate(keys, axis=0), query, preferred_element_type=f32)

    def gather(slot, index, which, scores, shift):
        raised = jnp.exp(scores - shift).astype(bf16)
        picked = jnp.concatenate([slot[1][:, pl.ds(place, BLK)] for place in places(index, which)], axis=1)
        return jnp.dot(jnp.concatenate([picked, ones], axis=0), raised, preferred_element_type=f32)

    def by_head(rows):
        return jnp.where(row < HD, rows[:, :BLK], rows[:, BLK:])

    def finish(half, index, shift, total, rescale=None):
        mine = jnp.concatenate([total[:HD, :BLK], total[HD:LANES, BLK:]], axis=0)
        count_all = total[LANES : LANES + 1]
        span = slice(half * LANES, (half + 1) * LANES)
        if not first:
            before = sum_in_ref[span, at(index)]
            count_before = row_in_ref[half, 1:2, at(index, 2 * BLK)]
            if rescale is not None:
                before = before * by_head(rescale)
                count_before = count_before * rescale
            mine = mine + before
            count_all = count_all + count_before
        if last:
            out_ref[at(index), span] = (mine * by_head(1.0 / count_all)).T.astype(bf16)
        else:
            sum_out_ref[span, at(index)] = mine
            row_out_ref[half, 0:1, at(index, 2 * BLK)] = shift
            row_out_ref[half, 1:2, at(index, 2 * BLK)] = count_all
        return count_all

    def one(half, index):
        query = queries(half, index)
        slot = slots[half]
        total = None
        shift = None if first else row_in_ref[half, 0:1, at(index, 2 * BLK)]
        for which in range(0, count, 2):
            scores = score(slot, index, which, query)
            if shift is None:
                shift = jnp.max(scores, axis=0, keepdims=True)
            part = gather(slot, index, which, scores, shift)
            total = part if total is None else total + part
        return finish(half, index, shift, total)

    def whole_row(half, index):
        query = queries(half, index)
        slot = slots[half]
        shift = jnp.full((1, 2 * BLK), -jnp.inf, f32) if first else row_in_ref[half, 0:1, at(index, 2 * BLK)]
        old = shift

        def largest(n, shift):
            return jnp.maximum(shift, jnp.max(score(slot, index, 2 * n, query), axis=0, keepdims=True))

        shift = lax.fori_loop(0, count // 2, largest, shift)

        def add(n, total):
            return total + gather(slot, index, 2 * n, score(slot, index, 2 * n, query), shift)

        total = lax.fori_loop(0, count // 2, add, jnp.zeros((LANES + 16, 2 * BLK), f32))
        finish(half, index, shift, total, None if first else jnp.exp(old - shift))

    step = pl.program_id(0)
    steps = pl.num_programs(0)
    together = 2 if blocks % 2 == 0 else 1

    def attend_pair(half, following):
        def body(number, peak):
            for n in range(together):
                index = number * together + n
                if following is not None:
                    project(following, index, slots[1 - half])
                peak = jnp.maximum(peak, one(half, index))
            return peak

        return lax.fori_loop(0, blocks // together, body, jnp.zeros((1, 2 * BLK), f32))

    def repair(half, peak):
        @pl.when(jnp.logical_not(jnp.max(peak) <= TOTAL_CAP))
        def _():
            lax.fori_loop(0, blocks, lambda index, carry: (whole_row(half, index), carry)[1], 0)

    @pl.when(step == 0)
    def _():
        lax.fori_loop(0, blocks, lambda index, carry: (project(0, index, slots[0]), carry)[1], 0)

    repair(0, attend_pair(0, 2 * step + 1))

    @pl.when(step < steps - 1)
    def _():
        repair(1, attend_pair(1, 2 * step + 2))

    @pl.when(step == steps - 1)
    def _():
        repair(1, attend_pair(1, None))


def attend(name, table, query, weight, sources, state, last):
    f32, bf16 = jnp.float32, jnp.bfloat16
    rows = query.shape[1]
    blocks = rows // BLK
    count = table.shape[1]
    total_rows = sum(source.shape[0] for source in sources)
    whole = lambda array: pl.BlockSpec(array.shape, lambda g: (0, 0), pipeline_mode=pl.Buffered(1))
    columns = pl.BlockSpec((2 * LANES, rows), lambda g: (g, 0))
    per_row = pl.BlockSpec((2, 2, 2 * rows), lambda g: (g, 0, 0))
    in_specs = [pl.BlockSpec(memory_space=pltpu.SMEM), columns, whole(weight)]
    in_specs += [whole(source) for source in sources]
    if state:
        in_specs += [columns, per_row]
    if last:
        out_specs = pl.BlockSpec((rows, 2 * LANES), lambda g: (0, g))
        out_shape = jax.ShapeDtypeStruct((rows, D), bf16)
    else:
        out_specs = [columns, per_row]
        out_shape = [jax.ShapeDtypeStruct((D, rows), f32), jax.ShapeDtypeStruct((PAIRS, 2, 2 * rows), f32)]
    scores = rows * count * BLK * H
    return pl.pallas_call(
        functools.partial(attend_kernel, not state, last, blocks, count, len(sources)),
        grid=(PAIRS // 2,),
        in_specs=in_specs,
        out_specs=out_specs,
        out_shape=out_shape,
        scratch_shapes=[pltpu.VMEM((total_rows, LANES), bf16), pltpu.VMEM((LANES, total_rows), bf16)] * 2,
        compiler_params=pltpu.CompilerParams(vmem_limit_bytes=48 * 2**20),
        cost_estimate=pl.CostEstimate(
            flops=16 * scores * HD + 4 * total_rows * D * D,
            bytes_accessed=2 * (total_rows * D + weight.size + query.size) + 8 * rows * D,
            transcendentals=scores,
        ),
        name=name,
    )(table, query, weight, *sources, *state)


def on_device(tokens, proj_weight, out_weight, pattern):
    heads = lax.axis_size("head")
    strides = lax.axis_size("blk")
    place = lax.axis_index("head")
    stride = lax.axis_index("blk")
    own = tokens[0]
    blocks = own.shape[0] // BLK
    lower = place < heads // 2
    summary = SUMB * BLK
    share = summary // heads

    along = []
    for h in range(heads):
        for s in range(strides - 1):
            ends = (h * strides + s, h * strides + s + 1)
            along.append(ends if h < heads // 2 else ends[::-1])
    to_next = lambda rows: lax.ppermute(rows, ("head", "blk"), along)

    if heads == 2:
        swap = lambda rows: lax.ppermute(rows, "head", [(0, 1), (1, 0)])
        cut = own.shape[0] - summary
        other_mid = swap(own[cut : cut + share])
        piece = jnp.where(lower, other_mid, own[cut + share :])
        far_rows = lax.all_gather(piece, ("blk", "head"), axis=0, tiled=True)
        other_low = swap(own[:cut])
        other_high = jnp.concatenate([other_mid, swap(own[cut + share :])], axis=0)
        other = jnp.concatenate([other_low, other_high], axis=0)
        edge = jnp.concatenate([to_next(other_low), to_next(other_high)], axis=0)
        near_rows = [own, other, edge]
    else:
        stride_rows = lax.all_gather(own, "head", axis=0, tiled=True)
        piece = lax.dynamic_slice_in_dim(stride_rows[-summary:], place * share, share, 0)
        far_rows = lax.all_gather(piece, ("blk", "head"), axis=0, tiled=True)
        half = stride_rows.shape[0] // 2
        near_rows = [stride_rows, to_next(jnp.where(lower, stride_rows[half:], stride_rows[:half]))]

    query_weight, weight = split_weights(proj_weight)
    query = lax.dot_general(query_weight, own, (((1,), (1,)), ((), ())), preferred_element_type=jnp.float32)
    query = (query * HD**-0.5).astype(jnp.bfloat16)

    listed = lax.dynamic_slice_in_dim(pattern, place * blocks, blocks, 0)
    near = listed[:, :LSEL] - stride * SB
    swapped = jnp.logical_and(heads == 2, jnp.logical_and(jnp.logical_not(lower), near < SB))
    near = jnp.where(near < 0, near + SB + REACH, jnp.where(swapped, near ^ (SB // 2), near))
    far = listed[:, LSEL:]
    far = far // SB * SUMB + far % SB - (SB - SUMB)

    state = attend("attend_far", far, query, weight, [far_rows], [], False)
    mixed = attend("attend_near", near, query, weight, near_rows, state, True)
    out = jnp.dot(mixed, out_weight, preferred_element_type=jnp.float32).astype(jnp.bfloat16)
    return out.reshape(tokens.shape)


def solution(mesh):
    return jax.shard_map(
        on_device,
        mesh=mesh,
        in_specs=(P(("batch", "blk"), "head", None), P(), P(), P(("batch", "blk"), None)),
        out_specs=P(("batch", "blk"), "head", None),
        check_vma=False,
    )
```

time: 1150 us -> 566 us (0.49)
  the two profiles are of different devices: /device:TPU:11 before, /device:TPU:23 now
where the time goes in v2:
time: 566 us; the launch traced here: 577 us
  Pallas kernels  449 us (79%)
  waiting for transfers between devices  77.6 us (14%)
  between operations  13.4 us (2%)
  starting transfers between devices  12 us (2%)
  matrix products  9.54 us (2%)
  other arithmetic  8.76 us (2%)
  local copies, waits for them, and re-layouts  6.11 us (1%)
    pallas_call x2, Pallas kernels, attend(): pl.pallas_call(functools.partial(attend_kernel, not state, last, blocks,...  441 us
    ppermute x3, waiting for transfers between devices, on_device(): swap = lambda rows: lax.ppermute(rows, 'head', [(0, 1), (1, 0)])  53.4 us
    ppermute x2, waiting for transfers between devices, on_device(): to_next = lambda rows: lax.ppermute(rows, ('head', 'blk'), along)  24.2 us
  transfers between devices with their start and end apart: 6, of which 4 were waited for; matrix products, arithmetic and copies ran while one was open for 3% of the time, Pallas kernels for 1%

profile of v2, /device:TPU:23, one launch (start us, length us, event | category | flops | bytes accessed | tf_op | source)
XLA Modules:
  0.0 576.5 jit_solution(4213154893636143499)
XLA Ops:
  6.5 0.0 copy-start
  6.5 0.0 all-gather.2.cloned.1.call-start
  6.5 2.2 slice_bitcast_fusion.2
  8.8 0.2 collective-permute-start.1
  9.0 0.0 copy-start.2
  9.0 12.6 %collective-permute-done.1 = bf16[256,1024]{1,0:T(8,128)(2,1)S(1)} collective-permute-done((bf16[256,1024]{1,0:T(8,128)(2,1)S(1)}, bf16[256,1024]{1,0:T(8,128)(2,1)S(1)}, u32[]{:S(2)}, u32[]{:S(2)}) %collective-permute-start.1) | collective-permute-done | bytes 524320 | tf_op jit(solution)/shard_map/ppermute | solution.py:265
  21.6 1.9 broadcast_select_fusion
  23.5 0.0 all-gather.2.cloned.1.call-update
  23.5 2.3 slice_bitcast_fusion
  25.8 0.2 collective-permute-start
  26.0 1.2 collective-permute-start.2
  27.3 0.0 copy-done.2
  27.3 40.8 %collective-permute-done.2 = bf16[256,1024]{1,0:T(8,128)(2,1)S(1)} collective-permute-done((bf16[256,1024]{1,0:T(8,128)(2,1)}, bf16[256,1024]{1,0:T(8,128)(2,1)S(1)}, u32[]{:S(2)}, u32[]{:S(2)}) %collective-permute-start.2) | collective-permute-done | bytes 524320 | tf_op jit(solution)/shard_map/ppermute | solution.py:265
  68.1 1.0 pad_maximum_fusion.2
  69.1 8.4 %collective-permute-start.4 = (bf16[512,1024]{1,0:T(8,128)(2,1)}, bf16[512,1024]{1,0:T(8,128)(2,1)}, u32[]{:S(2)}, u32[]{:S(2)}) collective-permute-start(bf16[512,1024]{1,0:T(8,128)(2,1)} %pad_maximum_fusion.2), channel_id=1, source_target_pairs={{0,1},{1,2},{2,3},{3,4},{4,5},{5,6},{6,7},{9,8},{10,9},{11,10},{12... | collective-permute-start | bytes 3145736 | tf_op jit(solution)/shard_map/ppermute | solution.py:262
  77.5 0.0 collective-permute-done
  77.5 1.9 collective-permute-start.3
  79.4 0.1 fusion.3.refs_0_
  79.5 8.4 %split_weights.1 = (bf16[1024,1024]{1,0:T(8,128)(2,1)}, bf16[1024,2048]{1,0:T(8,128)(2,1)}) custom-call(bf16[1024,3072]{1,0:T(8,128)(2,1)} %weight_ref.1), custom_call_target="tpu_custom_call" | custom-call | bytes 12582912 | tf_op jit(solution)/shard_map/split_weights/pallas_call | solution.py:38
  88.0 5.9 %multiply_convert_fusion.refs_1_ = bf16[1024,1024]{1,0:T(8,128)(2,1)} fusion(bf16[1024,1024]{1,0:T(8,128)(2,1)} %get-tuple-element.9, bf16[1,1024,1024]{2,1,0:T(8,128)(2,1)} %param.4), kind=kOutput, calls=%fused_computation | convolution fusion | flops 2149580800 | bytes 6291456 | tf_op jit(solution)/shard_map/dot_general | solution.py:283
  93.9 2.7 pad_maximum_fusion.refs_4_
  96.6 11.6 %collective-permute-done.4 = bf16[512,1024]{1,0:T(8,128)(2,1)} collective-permute-done((bf16[512,1024]{1,0:T(8,128)(2,1)}, bf16[512,1024]{1,0:T(8,128)(2,1)}, u32[]{:S(2)}, u32[]{:S(2)}) %collective-permute-start.4) | collective-permute-done | bytes 1048608 | tf_op jit(solution)/shard_map/ppermute | solution.py:262
  108.2 12.6 %collective-permute-done.3 = bf16[512,1024]{1,0:T(8,128)(2,1)} collective-permute-done((bf16[512,1024]{1,0:T(8,128)(2,1)}, bf16[512,1024]{1,0:T(8,128)(2,1)}, u32[]{:S(2)}, u32[]{:S(2)}) %collective-permute-start.3) | collective-permute-done | bytes 1048608 | tf_op jit(solution)/shard_map/ppermute | solution.py:262
  120.8 3.0 pad_maximum_fusion.1.refs_5_
  123.8 0.0 all-gather.2.cloned.1.call-done.refs_3_
  123.8 0.0 copy-start.1
  123.8 1.6 copy-done.1
  125.4 267.6 %attend_far.1 = (f32[1024,1024]{1,0:T(8,128)}, f32[8,2,2048]{2,1,0:T(2,128)S(1)}) custom-call(s32[8,10]{1,0:T(8,128)S(1)} %fusion.3.refs_0_, bf16[1024,1024]{1,0:T(8,128)(2,1)S(1)} %copy-done.1, bf16[1024,2048]{1,0:T(8,128)(2,1)} %get-tuple-element.10.refs_2_, bf16[4096,1024]{1,0:T(8,128)(2,1)} %all-gather.2.cloned.1.call-done.refs_3_), custom_call_target="tpu_custom_call" | custom-call | flops 38654705664 | bytes 23068672 | tf_op jit(solution)/shard_map/attend_far/pallas_call | solution.py:229
  392.9 173.1 %attend_near.1 = bf16[1024,1024]{1,0:T(8,128)(2,1)S(1)} custom-call(s32[8,6]{1,0:T(8,128)S(1)} %fusion.refs_0_, bf16[1024,1024]{1,0:T(8,128)(2,1)S(1)} %copy-done.1, bf16[1024,2048]{1,0:T(8,128)(2,1)} %get-tuple-element.10.refs_2_, bf16[1024,1024]{1,0:T(8,128)(2,1)} %bitcast.16, bf16[1024,1024]{1,0:T(8,128)(2,1)} %pad_maximum_fusion.refs_4_, ...), custom_call_target="tpu_custom_call" | custom-call | flops 25769803776 | bytes 20971520 | tf_op jit(solution)/shard_map/attend_near/pallas_call | solution.py:229
  566.0 0.0 copy-done
  566.0 3.7 convert_bitcast_fusion
  (2 shorter events, 0.0 us)
Async XLA Ops:
  6.5 559.5 %copy-start = (bf16[1024,1024]{1,0:T(8,128)(2,1)S(1)}, bf16[1024,1024]{1,0:T(8,128)(2,1)}, u32[]{:S(2)}) copy-start(bf16[1024,1024]{1,0:T(8,128)(2,1)} %param.6) | copy-start | bytes 6291460
  6.5 117.3 %all-gather.2.cloned.1.call-start = ((), (), s32[]{:S(2)}) async-start(), calls=%async_computation | async-start | bytes 8912896 | tf_op jit(solution)/shard_map/all_gather | solution.py:269
  8.8 12.8 %collective-permute-start.1 = (bf16[256,1024]{1,0:T(8,128)(2,1)S(1)}, bf16[256,1024]{1,0:T(8,128)(2,1)S(1)}, u32[]{:S(2)}, u32[]{:S(2)}) collective-permute-start(bf16[256,1024]{1,0:T(8,128)(2,1)S(1)} %get-tuple-element.13), channel_id=1, source_target_pairs={{0,8},{8,0},{1,9},{9,1},{2,10},{10,2},{3,11},{11,3},{4,12},{12,4},... | collective-permute-start | bytes 1572872 | tf_op jit(solution)/shard_map/ppermute | solution.py:265
  9.0 18.3 %copy-start.2 = (s32[16,16]{1,0:T(8,128)S(1)}, s32[16,16]{1,0:T(8,128)}, u32[]{:S(2)}) copy-start(s32[16,16]{1,0:T(8,128)} %param.7) | copy-start | bytes 3076
  25.8 51.7 %collective-permute-start = (bf16[512,1024]{1,0:T(8,128)(2,1)}, bf16[512,1024]{1,0:T(8,128)(2,1)}, u32[]{:S(2)}, u32[]{:S(2)}) collective-permute-start(bf16[512,1024]{1,0:T(8,128)(2,1)} %slice_bitcast_fusion), channel_id=1, source_target_pairs={{0,8},{8,0},{1,9},{9,1},{2,10},{10,2},{3,11},{11,3},{4,12},{12,4},... | collective-permute-start | bytes 3145736 | tf_op jit(solution)/shard_map/ppermute | solution.py:265
  26.0 42.0 %collective-permute-start.2 = (bf16[256,1024]{1,0:T(8,128)(2,1)}, bf16[256,1024]{1,0:T(8,128)(2,1)S(1)}, u32[]{:S(2)}, u32[]{:S(2)}) collective-permute-start(bf16[256,1024]{1,0:T(8,128)(2,1)} %get-tuple-element.14), channel_id=1, source_target_pairs={{0,8},{8,0},{1,9},{9,1},{2,10},{10,2},{3,11},{11,3},{4,12},{12,4},... | collective-permute-start | bytes 1572872 | tf_op jit(solution)/shard_map/ppermute | solution.py:265
  69.1 39.1 %collective-permute-start.4 = (bf16[512,1024]{1,0:T(8,128)(2,1)}, bf16[512,1024]{1,0:T(8,128)(2,1)}, u32[]{:S(2)}, u32[]{:S(2)}) collective-permute-start(bf16[512,1024]{1,0:T(8,128)(2,1)} %pad_maximum_fusion.2), channel_id=1, source_target_pairs={{0,1},{1,2},{2,3},{3,4},{4,5},{5,6},{6,7},{9,8},{10,9},{11,10},{12... | collective-permute-start | bytes 3145736 | tf_op jit(solution)/shard_map/ppermute | solution.py:262
  77.5 43.3 %collective-permute-start.3 = (bf16[512,1024]{1,0:T(8,128)(2,1)}, bf16[512,1024]{1,0:T(8,128)(2,1)}, u32[]{:S(2)}, u32[]{:S(2)}) collective-permute-start(bf16[512,1024]{1,0:T(8,128)(2,1)} %collective-permute-done), channel_id=1, source_target_pairs={{0,1},{1,2},{2,3},{3,4},{4,5},{5,6},{6,7},{9,8},{10,9},{11,10},{12... | collective-permute-start | bytes 3145736 | tf_op jit(solution)/shard_map/ppermute | solution.py:262
  123.8 1.6 copy-start.1
Sparse Core Ops, SparseCore 0:
  23.7 88.8 all-gather.1
